TPU v7x, 32 devices: a whole 2x2x4 slice. The times are simulated.
32 devices in a mesh: parts: 2 (over y), tensor: 4 (over z), dp: 4 (over x, core).
Axes of the slice: x: 2, y: 2, z: 4, core: 2. Of those that a mesh axis runs over, the one named last changes fastest.
Arguments:
- layer_input: bfloat16 [2048, 4096], P(('parts', 'tensor'), 'dp'), parts along dimension 0, may hold values from -6 to 6
- gate_pre: bfloat16 [2048, 16384], P(('parts', 'dp'), 'tensor'), parts along dimension 0, may hold values from -8 to 8
- up_pre: bfloat16 [2048, 16384], P(('parts', 'dp'), 'tensor'), parts along dimension 0, may hold values from -6 to 6
- d_hidden: bfloat16 [2048, 16384], P(('parts', 'dp'), 'tensor'), parts along dimension 0, may hold values from -2 to 2
- w_gate: bfloat16 [4096, 16384], P('dp', 'tensor'), may hold values from -0.09375 to 0.09375
- w_up: bfloat16 [4096, 16384], P('dp', 'tensor'), may hold values from -0.09375 to 0.09375
- mask_gate: int32 [32, 128], P('dp', 'tensor'), may hold values 0 or 1
- mask_up: int32 [32, 128], P('dp', 'tensor'), may hold values 0 or 1
- lengths: int32 [8], P('parts'), parts along dimension 0, may hold values from 112 to 256, as said below
Outputs:
- input_grad: bfloat16 [2048, 4096], P(('parts', 'tensor'), 'dp'), parts along dimension 0
- grad_w_gate: bfloat16 [8192, 16384], P(('parts', 'dp'), 'tensor'), parts along dimension 0
- grad_w_up: bfloat16 [8192, 16384], P(('parts', 'dp'), 'tensor'), parts along dimension 0
There are 2 independent parts, one for each index of `parts`. A program takes and returns all parts, laid end to end along the dimension named above; an argument that names none is the same for every part. Nothing has to cross between parts.
Inputs may be any that keep to these rules, and one draw needn't show every extreme that they name: Groups g and g + 4/2 form a pair whose lengths sum to at most 384; in every draw some group has all 256 slots used.
All inputs are finite; a program needn't handle non-finite values. No bound on the sum of `mask_gate` or of `mask_up` on one device may be relied on, other than what follows from the above.
Results may differ from a plain program's by a relative error of at most 0.0095.
Values may be sent and summed in bfloat16 or wider, within the bound.
A program may use at most 192 MiB of HBM per device.

v0:
```python
import jax
import jax.numpy as jnp
from jax import lax
from jax.sharding import PartitionSpec as P

BLK = 128


def expand(mask):
    return jnp.repeat(jnp.repeat(mask, BLK, axis=0), BLK, axis=1)


def swiglu_back(gate, upper, grad, keep):
    g = gate.astype(jnp.float32)
    sig = jax.nn.sigmoid(g)
    err = jnp.where(keep[:, None], grad.astype(jnp.float32), jnp.float32(0.0))
    d_up = err * g * sig
    d_gate = err * upper.astype(jnp.float32) * sig * (1.0 + g * (1.0 - sig))
    return (d_gate.astype(jnp.bfloat16), d_up.astype(jnp.bfloat16))


def local(layer_input, gate_pre, up_pre, d_hidden, w_gate, w_up, mask_gate, mask_up, lengths):
    group = lax.axis_index("dp")
    slots_dev = gate_pre.shape[0]
    keep_gate = expand(mask_gate).astype(jnp.bfloat16)
    keep_up = expand(mask_up).astype(jnp.bfloat16)
    gate_eff = w_gate * keep_gate
    up_eff = w_up * keep_up
    inner = (((1,), (1,)), ((), ()))
    input_all = lax.all_gather(layer_input, "tensor", axis=0, tiled=True)
    keep = jnp.arange(slots_dev) < lengths[group]
    d_gate, d_up = swiglu_back(gate_pre, up_pre, d_hidden, keep)
    gate_all, up_all = (
        lax.all_gather(d_gate, "dp", axis=0, tiled=True),
        lax.all_gather(d_up, "dp", axis=0, tiled=True),
    )
    term = lax.dot_general(gate_all, gate_eff, inner, preferred_element_type=jnp.float32)
    summed = lax.psum_scatter(
        (term + lax.dot_general(up_all, up_eff, inner, preferred_element_type=jnp.float32)).astype(
            jnp.bfloat16
        ),
        "tensor",
        scatter_dimension=0,
        tiled=True,
    )
    contract = (((0,), (0,)), ((), ()))
    grad_w_gate = lax.dot_general(input_all, gate_all, contract, preferred_element_type=jnp.float32)
    grad_w_gate = (grad_w_gate * keep_gate.astype(jnp.float32)).astype(jnp.bfloat16)
    grad_w_up = lax.dot_general(input_all, up_all, contract, preferred_element_type=jnp.float32)
    grad_w_up = (grad_w_up * keep_up.astype(jnp.float32)).astype(jnp.bfloat16)
    return (summed, grad_w_gate, grad_w_up)


def solution(mesh):
    placed = (
        P(("parts", "tensor"), "dp"),
        P(("parts", "dp"), "tensor"),
        P(("parts", "dp"), "tensor"),
        P(("parts", "dp"), "tensor"),
        P("dp", "tensor"),
        P("dp", "tensor"),
        P("dp", "tensor"),
        P("dp", "tensor"),
        P("parts"),
    )
    return jax.shard_map(
        local,
        mesh=mesh,
        in_specs=placed,
        out_specs=(
            P(("parts", "tensor"), "dp"),
            P(("parts", "dp"), "tensor"),
            P(("parts", "dp"), "tensor"),
        ),
        check_vma=False,
    )
```

profile of v0, /device:TPU:0, one launch (start us, length us, event | category | flops | bytes accessed | tf_op | source)
XLA Modules:
  0.0 243.4 jit_solution(5815315445881964274)
XLA Ops:
  7.2 0.0 copy-start
  7.2 0.0 all-gather.4.cloned.1.call-start
  7.2 1.2 dynamic_slice.3
  8.5 0.6 iota_compare_fusion
  9.1 5.7 %fusion.9 = (bf16[256,4096]{1,0:T(8,128)(2,1)}, bf16[256,4096]{1,0:T(8,128)(2,1)}) fusion(bf16[256,4096]{1,0:T(8,128)(2,1)} %param.10, bf16[256,4096]{1,0:T(8,128)(2,1)} %param.12, pred[256]{0:T(512)(128)(4,1)S(1)} %iota_compare_fusion, bf16[256,4096]{1,0:T(8,128)(2,1)} %param.11), kind=kLoop, calls=%fused_computation.16 | loop fusion | flops 17825792 | bytes 10486016 | tf_op jit(solution)/shard_map/convert_element_type | solution.py:19
  14.8 0.0 all-gather.4.cloned.1.call-update
  14.9 0.0 all-gather.6.cloned.1.call-start
  14.9 0.7 all-gather.6.cloned.1.call-update
  15.6 0.0 all-gather.8.cloned.1.call-start
  15.7 0.7 all-gather.8.cloned.1.call-update
  16.4 0.0 reduce-scatter.2.cloned.1.call-start
  16.4 0.0 copy-done
  16.4 0.1 copy.12
  16.5 0.1 broadcast_in_dim.27
  16.6 0.0 copy-start.1
  16.7 12.2 %copy.13 = bf16[1024,4096]{0,1:T(8,128)(2,1)} copy(bf16[1024,4096]{1,0:T(8,128)(2,1)} %param.13) | data formatting | bytes 16777216 | tf_op args[4]
  28.8 0.1 copy.14
  28.9 0.1 broadcast_in_dim.29
  29.0 12.0 %copy.15 = bf16[1024,4096]{0,1:T(8,128)(2,1)} copy(bf16[1024,4096]{1,0:T(8,128)(2,1)} %param.14) | data formatting | bytes 16777216 | tf_op args[5]
  41.1 7.4 %bitcast_multiply_fusion.3 = bf16[1024,4096]{0,1:T(8,128)(2,1)} fusion(bf16[1024,4096]{0,1:T(8,128)(2,1)} %copy.13, bf16[1024,32]{0,1:T(8,128)(2,1)S(1)} %bitcast.35), kind=kLoop, calls=%fused_computation.5 | loop fusion | flops 4194304 | bytes 16842752 | tf_op jit(solution)/shard_map/mul | solution.py:27
  48.5 7.3 %bitcast_multiply_fusion.2 = bf16[1024,4096]{0,1:T(8,128)(2,1)} fusion(bf16[1024,4096]{0,1:T(8,128)(2,1)} %copy.15, bf16[1024,32]{0,1:T(8,128)(2,1)S(1)} %bitcast.37), kind=kLoop, calls=%fused_computation.4 | loop fusion | flops 4194304 | bytes 16842752 | tf_op jit(solution)/shard_map/mul | solution.py:28
  55.8 20.2 %all-gather.4.cloned.1.call-done = bf16[1024,4096]{1,0:T(8,128)(2,1)} async-done(((bf16[256,4096]{1,0:T(8,128)(2,1)}), bf16[1024,4096]{1,0:T(8,128)(2,1)}) %all-gather.4.cloned.1.call-update) | async-done | bytes 8388624 | tf_op jit(solution)/shard_map/all_gather | solution.py:34
  76.0 15.0 %fusion.10 = f32[1024,1024]{1,0:T(8,128)} fusion(bf16[1024,4096]{1,0:T(8,128)(2,1)} %all-gather.4.cloned.1.call-done, bf16[1024,4096]{0,1:T(8,128)(2,1)} %bitcast_multiply_fusion.3), kind=kOutput, calls=%fused_computation.22 | convolution fusion | flops 8589934592 | bytes 20971520 | tf_op jit(solution)/shard_map/dot_general | solution.py:37
  91.0 44.9 %all-gather.6.cloned.1.call-done = bf16[1024,4096]{1,0:T(8,128)(2,1)} async-done(((bf16[256,4096]{1,0:T(8,128)(2,1)}), bf16[1024,4096]{1,0:T(8,128)(2,1)}) %all-gather.6.cloned.1.call-update) | async-done | bytes 8388624 | tf_op jit(solution)/shard_map/all_gather | solution.py:35
  135.9 15.3 %add_convert_fusion = bf16[1024,1024]{1,0:T(8,128)(2,1)} fusion(f32[1024,1024]{1,0:T(8,128)} %fusion.10, bf16[1024,4096]{1,0:T(8,128)(2,1)} %all-gather.6.cloned.1.call-done, bf16[1024,4096]{0,1:T(8,128)(2,1)} %bitcast_multiply_fusion.2), kind=kOutput, calls=%fused_computation.17 | convolution fusion | flops 8592031744 | bytes 23068672 | tf_op jit(solution)/shard_map/dot_general | solution.py:39
  151.2 0.0 reduce-scatter.2.cloned.1.call-update
  151.2 32.2 %all-gather.8.cloned.1.call-done = bf16[1024,1024]{1,0:T(8,128)(2,1)} async-done(((bf16[256,1024]{1,0:T(8,128)(2,1)}), bf16[1024,1024]{1,0:T(8,128)(2,1)}) %all-gather.8.cloned.1.call-update) | async-done | bytes 2097168 | tf_op jit(solution)/shard_map/all_gather | solution.py:30
  183.4 14.9 %fusion.1 = bf16[1024,4096]{0,1:T(8,128)(2,1)} fusion(bf16[1024,4096]{1,0:T(8,128)(2,1)} %all-gather.4.cloned.1.call-done, bf16[1024,1024]{1,0:T(8,128)(2,1)} %all-gather.8.cloned.1.call-done, bf16[1024,32]{0,1:T(8,128)(2,1)S(1)} %bitcast.36), kind=kOutput, calls=%fused_computation.3 | convolution fusion | flops 8602517504 | bytes 18939904 | tf_op jit(solution)/shard_map/dot_general | solution.py:47
  198.3 12.1 %copy.16 = bf16[1024,4096]{1,0:T(8,128)(2,1)} copy(bf16[1024,4096]{0,1:T(8,128)(2,1)} %fusion.1) | data formatting | bytes 16777216
  210.4 0.0 copy-done.2
  210.4 14.6 %fusion = bf16[1024,4096]{0,1:T(8,128)(2,1)} fusion(bf16[1024,4096]{1,0:T(8,128)(2,1)} %all-gather.6.cloned.1.call-done, bf16[1024,1024]{1,0:T(8,128)(2,1)S(1)} %copy-done.2, bf16[1024,32]{0,1:T(8,128)(2,1)S(1)} %bitcast.38), kind=kOutput, calls=%fused_computation.1 | convolution fusion | flops 8602517504 | bytes 18939904 | tf_op jit(solution)/shard_map/dot_general | solution.py:49
  225.0 11.9 %copy.17 = bf16[1024,4096]{1,0:T(8,128)(2,1)} copy(bf16[1024,4096]{0,1:T(8,128)(2,1)} %fusion) | data formatting | bytes 16777216
  (7 shorter events, 0.0 us)
Async XLA Ops:
  7.2 9.2 %copy-start = (s32[8,32]{1,0:T(8,128)S(1)}, s32[8,32]{1,0:T(8,128)}, u32[]{:S(2)}) copy-start(s32[8,32]{1,0:T(8,128)} %param.15) | copy-start | bytes 3076
  7.2 68.8 %all-gather.4.cloned.1.call-start = ((), (), s32[]{:S(2)}) async-start(), calls=%async_computation.1 | async-start | bytes 10485760 | tf_op jit(solution)/shard_map/all_gather | solution.py:34
  14.9 121.0 %all-gather.6.cloned.1.call-start = ((), (), s32[]{:S(2)}) async-start(), calls=%async_computation.2 | async-start | bytes 10485760 | tf_op jit(solution)/shard_map/all_gather | solution.py:35
  15.6 167.8 %all-gather.8.cloned.1.call-start = ((), (), s32[]{:S(2)}) async-start(), calls=%async_computation.4 | async-start | bytes 2621440 | tf_op jit(solution)/shard_map/all_gather | solution.py:30
  16.4 220.6 %reduce-scatter.2.cloned.1.call-start = ((), (), s32[]{:S(2)}) async-start(), calls=%async_computation.3 | async-start | bytes 2621440 | tf_op jit(solution)/shard_map/reduce_scatter | solution.py:38
  16.6 12.2 %copy-start.1 = (s32[8,32]{1,0:T(8,128)S(1)}, s32[8,32]{1,0:T(8,128)}, u32[]{:S(2)}) copy-start(s32[8,32]{1,0:T(8,128)} %param.16) | copy-start | bytes 3076
  198.3 12.1 %copy-start.2 = (bf16[1024,1024]{1,0:T(8,128)(2,1)S(1)}, bf16[1024,1024]{1,0:T(8,128)(2,1)}, u32[]{:S(2)}) copy-start(bf16[1024,1024]{1,0:T(8,128)(2,1)} %all-gather.8.cloned.1.call-done) | copy-start | bytes 6291460
Sparse Core Ops, SparseCore 0:
  15.0 60.9 all-gather.3
  77.6 58.2 all-gather.5
  137.5 45.8 all-gather.7
  186.1 42.6 reduce-scatter.1
where the time goes:
time: 245 us; the launch traced here: 243 us
  waiting for transfers between devices  98.7 us (40%)
  matrix products  59.8 us (24%)
  local copies, waits for them, and re-layouts  49.8 us (20%)
  other arithmetic  21.1 us (9%)
  between operations  13.8 us (6%)
    unnamed x12, local copies, waits for them, and re-layouts  48.2 us
    all_gather x1, waiting for transfers between devices, local(): lax.all_gather(d_up, 'dp', axis=0, tiled=True)  44.9 us
    all_gather x1, waiting for transfers between devices, local(): input_all = lax.all_gather(layer_input, 'tensor', axis=0, tiled=True)  32.2 us
    all_gather x1, waiting for transfers between devices, local(): lax.all_gather(d_gate, 'dp', axis=0, tiled=True)  20.2 us
    dot_general x1, matrix products, local(): lax.dot_general(up_all, up_eff, inner, preferred_element_type=jnp.float32)  15.3 us
    dot_general x1, matrix products, local(): lax.dot_general(gate_all, gate_eff, inner, preferred_element_type=jnp.flo...  15 us
    dot_general x1, matrix products, local(): lax.dot_general(input_all, gate_all, contract, preferred_element_type=jnp...  14.9 us
    dot_general x1, matrix products, local(): lax.dot_general(input_all, up_all, contract, preferred_element_type=jnp.f...  14.6 us
  transfers between devices with their start and end apart: 4, of which 3 were waited for; matrix products, arithmetic and copies ran while one was open for 51% of the time, Pallas kernels for 0%

commit v1 on v0

--- a/solution.py
+++ b/solution.py
@@ -1,9 +1,298 @@
+import functools
+
 import jax
 import jax.numpy as jnp
 from jax import lax
+from jax.experimental import pallas as pl
+from jax.experimental.pallas import tpu as pltpu
 from jax.sharding import PartitionSpec as P
 
 BLK = 128
+STAGES = 4
+CORES = 2
+VMEM_LIMIT = 60 * 2**20
+MESH = pl.DeviceIdType.MESH
+NT = (((1,), (1,)), ((), ()))
+
+
+def gather_kernel(
+    x_in, gate_in, up_in, dh_in, wg_in, wu_in, mg_in, mu_in, len_in,
+    summed, dg_out, du_out, xt_out, kg_out, ku_out,
+    dg, du, wg, wu, gate, up, dh, xs, term, part,
+    load_sem, w_sem, x_sem, xsend, xrecv, psend, precv, ssend, srecv, fsend, frecv, out_sem, rsend, rrecv,
+):
+    t = lax.axis_index("tensor")
+    i = lax.axis_index("dp")
+    n_t = xs.shape[0] * xs.shape[2]
+    chip, core = i // CORES, i % CORES
+    far = 1 - chip
+    sib = chip * CORES + (1 - core)
+    pair = far * CORES + core
+    stages, rows, ff = gate.shape
+    feats = wg.shape[0]
+
+    loads = []
+    for r in range(stages):
+        loads.append([
+            pltpu.make_async_copy(src.at[r], dst.at[r], load_sem.at[r, k])
+            for k, (src, dst) in enumerate(((gate_in, gate), (up_in, up), (dh_in, dh)))
+        ])
+        for copy in loads[-1]:
+            copy.start()
+    w_loads = [
+        pltpu.make_async_copy(wg_in, wg, w_sem.at[0]),
+        pltpu.make_async_copy(wu_in, wu, w_sem.at[1]),
+    ]
+    for copy in w_loads:
+        copy.start()
+    own_x = pltpu.make_async_copy(x_in, xs.at[t // CORES, :, t % CORES], x_sem)
+    own_x.start()
+
+    barrier = pltpu.get_barrier_semaphore()
+    for peer in (sib, pair):
+        pl.semaphore_signal(barrier, inc=1, device_id={"dp": peer}, device_id_type=MESH)
+    for k in range(1, n_t):
+        pl.semaphore_signal(barrier, inc=1, device_id={"tensor": (t + k) % n_t}, device_id_type=MESH)
+    pl.semaphore_wait(barrier, n_t + 1)
+
+    x_copies = []
+    for k in range(1, n_t):
+        x_copies.append(pltpu.make_async_remote_copy(
+            src_ref=x_in,
+            dst_ref=xs.at[t // CORES, :, t % CORES],
+            send_sem=xsend.at[k - 1],
+            recv_sem=xrecv.at[k - 1],
+            device_id={"tensor": (t + k) % n_t},
+            device_id_type=MESH,
+        ))
+        x_copies[-1].start()
+
+    used = len_in[i]
+    p_copies, s_copies, f_copies = [], [], []
+    tile = min(512, ff)
+    for r in range(stages):
+        for copy in loads[r]:
+            copy.wait()
+
+        @pl.loop(0, ff // tile)
+        def _(c):
+            cols = pl.ds(pl.multiple_of(c * tile, tile), tile)
+            g = gate[r, :, cols].astype(jnp.float32)
+            sig = jax.nn.sigmoid(g)
+            slot = lax.broadcasted_iota(jnp.int32, (rows, tile), 0) + r * rows
+            err = jnp.where(slot < used, dh[r, :, cols].astype(jnp.float32), jnp.float32(0.0))
+            d_up = err * g * sig
+            d_gate = err * up[r, :, cols].astype(jnp.float32) * sig * (1.0 + g * (1.0 - sig))
+            dg[chip, r, core, :, cols] = d_gate.astype(jnp.bfloat16)
+            du[chip, r, core, :, cols] = d_up.astype(jnp.bfloat16)
+
+        for peer, send, recv, kept in ((pair, psend, precv, p_copies), (sib, ssend, srecv, s_copies)):
+            kept.append([
+                pltpu.make_async_remote_copy(
+                    src_ref=d.at[chip, r, core],
+                    dst_ref=d.at[chip, r, core],
+                    send_sem=send.at[r, k],
+                    recv_sem=recv.at[r, k],
+                    device_id={"dp": peer},
+                    device_id_type=MESH,
+                )
+                for k, d in enumerate((dg, du))
+            ])
+            for copy in kept[-1]:
+                copy.start()
+
+    blocks = mg_in.shape[1]
+    spread = (
+        lax.broadcasted_iota(jnp.int32, (blocks, ff), 1) // BLK
+        == lax.broadcasted_iota(jnp.int32, (blocks, ff), 0)
+    ).astype(jnp.float32)
+    for m_in, k_out, w, load in ((mg_in, kg_out, wg, w_loads[0]), (mu_in, ku_out, wu, w_loads[1])):
+        k_out[...] = jnp.dot(m_in[...].astype(jnp.float32), spread, preferred_element_type=jnp.float32)
+        load.wait()
+
+        @pl.loop(0, feats // BLK)
+        def _(a):
+            at = pl.ds(pl.multiple_of(a * BLK, BLK), BLK)
+            w[at, :] = w[at, :] * k_out[pl.ds(a, 1), :].astype(jnp.bfloat16)
+
+    out_copies = []
+
+    def stage(where, r):
+        for k, (d, d_out) in enumerate(((dg, dg_out), (du, du_out))):
+            copy = pltpu.make_async_copy(d.at[where, r], d_out.at[where, r], out_sem.at[where, r, k])
+            copy.start()
+            out_copies.append(copy)
+        wide = min(256, feats)
+
+        @pl.loop(0, feats // wide)
+        def _(n):
+            at = pl.ds(pl.multiple_of(n * wide, wide), wide)
+            total = lax.dot_general(
+                dg[where, r].reshape(CORES * rows, ff), wg[at, :], NT, preferred_element_type=jnp.float32
+            )
+            total = total + lax.dot_general(
+                du[where, r].reshape(CORES * rows, ff), wu[at, :], NT, preferred_element_type=jnp.float32
+            )
+            term[where, r, :, :, at] = total.astype(jnp.bfloat16).reshape(CORES, rows, wide)
+
+        for c in range(CORES):
+            owner = where * CORES + c
+
+            @pl.when(owner != t)
+            def _():
+                pltpu.make_async_remote_copy(
+                    src_ref=term.at[where, r, c],
+                    dst_ref=part.at[t, r],
+                    send_sem=rsend.at[owner, r],
+                    recv_sem=rrecv.at[t, r],
+                    device_id={"tensor": owner},
+                    device_id_type=MESH,
+                ).start()
+
+    for r in range(stages):
+        for copy in s_copies[r]:
+            copy.wait_recv()
+        stage(chip, r)
+
+    for r in range(stages):
+        for copy in p_copies[r]:
+            copy.wait_recv()
+        f_copies.append([
+            pltpu.make_async_remote_copy(
+                src_ref=d.at[far, r, core],
+                dst_ref=d.at[far, r, core],
+                send_sem=fsend.at[r, k],
+                recv_sem=frecv.at[r, k],
+                device_id={"dp": sib},
+                device_id_type=MESH,
+            )
+            for k, d in enumerate((dg, du))
+        ])
+        for copy in f_copies[-1]:
+            copy.start()
+        for copy in f_copies[-1]:
+            copy.wait_recv()
+        stage(far, r)
+        if r == stages - 2:
+            own_x.wait()
+            for copy in x_copies:
+                copy.wait_recv()
+            span = CORES * rows
+            for a in range(xs.shape[0]):
+                for b in range(stages):
+                    at = (a * stages + b) * span
+                    xt_out[:, at : at + span] = xs[a, b].reshape(span, feats).T
+
+    for k in range(1, n_t):
+        for r in range(stages):
+            other = (t + k) % n_t
+            copy = pltpu.make_async_remote_copy(
+                src_ref=term.at[other // CORES, r, other % CORES],
+                dst_ref=part.at[other, r],
+                send_sem=rsend.at[other, r],
+                recv_sem=rrecv.at[other, r],
+                device_id={"tensor": other},
+                device_id_type=MESH,
+            )
+            copy.wait_recv()
+            copy.wait_send()
+    for r in range(stages):
+        total = term[t // CORES, r, t % CORES].astype(jnp.float32)
+        for k in range(1, n_t):
+            total = total + part[(t + k) % n_t, r].astype(jnp.float32)
+        summed[r] = total.astype(jnp.bfloat16)
+
+    for copy in x_copies:
+        copy.wait_send()
+    for kept in (p_copies, s_copies, f_copies):
+        for copies in kept:
+            for copy in copies:
+                copy.wait_send()
+    for copy in out_copies:
+        copy.wait()
+
+
+def weight_kernel(xt, dg, du, kg, ku, out_g, out_u):
+    feats = xt.shape[0]
+    high = 256
+    for d, keep, out in ((dg, kg, out_g), (du, ku, out_u)):
+        for a in range(feats // high):
+            total = jnp.dot(xt[a * high : (a + 1) * high, :], d[...], preferred_element_type=jnp.float32)
+            for b in range(high // BLK):
+                row = a * (high // BLK) + b
+                out[row * BLK : (row + 1) * BLK, :] = (
+                    total[b * BLK : (b + 1) * BLK, :] * keep[row : row + 1, :]
+                ).astype(jnp.bfloat16)
+
+
+def staged(layer_input, gate_pre, up_pre, d_hidden, w_gate, w_up, mask_gate, mask_up, lengths):
+    slots, ff = gate_pre.shape
+    feats = w_gate.shape[0]
+    chips = lengths.shape[0] // CORES
+    rows = slots // STAGES
+    n_t = chips * CORES
+    bf16, f32 = jnp.bfloat16, jnp.float32
+    tokens = chips * CORES * slots
+
+    def cut(array):
+        return array.reshape(STAGES, rows, array.shape[1])
+
+    hbm = pl.BlockSpec(memory_space=pl.ANY)
+    vmem = pl.BlockSpec(memory_space=pltpu.VMEM)
+    dma = pltpu.SemaphoreType.DMA
+    summed, dg, du, xt, kg, ku = pl.pallas_call(
+        gather_kernel,
+        out_shape=(
+            jax.ShapeDtypeStruct((STAGES, rows, feats), bf16),
+            jax.ShapeDtypeStruct((chips, STAGES, CORES, rows, ff), bf16),
+            jax.ShapeDtypeStruct((chips, STAGES, CORES, rows, ff), bf16),
+            jax.ShapeDtypeStruct((feats, tokens), bf16),
+            jax.ShapeDtypeStruct((feats // BLK, ff), f32),
+            jax.ShapeDtypeStruct((feats // BLK, ff), f32),
+        ),
+        in_specs=[hbm] * 6 + [vmem] * 2 + [pl.BlockSpec(memory_space=pltpu.SMEM)],
+        out_specs=(vmem, hbm, hbm, vmem, vmem, vmem),
+        scratch_shapes=[
+            pltpu.VMEM((chips, STAGES, CORES, rows, ff), bf16),
+            pltpu.VMEM((chips, STAGES, CORES, rows, ff), bf16),
+            pltpu.VMEM((feats, ff), bf16),
+            pltpu.VMEM((feats, ff), bf16),
+            pltpu.VMEM((STAGES, rows, ff), bf16),
+            pltpu.VMEM((STAGES, rows, ff), bf16),
+            pltpu.VMEM((STAGES, rows, ff), bf16),
+            pltpu.VMEM((chips, STAGES, CORES, rows, feats), bf16),
+            pltpu.VMEM((chips, STAGES, CORES, rows, feats), bf16),
+            pltpu.VMEM((n_t, STAGES, rows, feats), bf16),
+            dma((STAGES, 3)), dma((2,)), dma, dma((n_t - 1,)), dma((n_t - 1,)),
+            dma((STAGES, 2)), dma((STAGES, 2)), dma((STAGES, 2)), dma((STAGES, 2)),
+            dma((STAGES, 2)), dma((STAGES, 2)), dma((chips, STAGES, 2)),
+            dma((n_t, STAGES)), dma((n_t, STAGES)),
+        ],
+        compiler_params=pltpu.CompilerParams(
+            collective_id=0, has_side_effects=True, vmem_limit_bytes=VMEM_LIMIT
+        ),
+        name="gather_and_input_grad",
+    )(
+        cut(layer_input), cut(gate_pre), cut(up_pre), cut(d_hidden),
+        w_gate, w_up, mask_gate, mask_up, lengths,
+    )
+    wide = 512
+    grad_w_gate, grad_w_up = pl.pallas_call(
+        weight_kernel,
+        grid=(ff // wide,),
+        out_shape=(jax.ShapeDtypeStruct((feats, ff), bf16),) * 2,
+        in_specs=[
+            pl.BlockSpec((feats, tokens), lambda j: (0, 0)),
+            pl.BlockSpec((tokens, wide), lambda j: (0, j)),
+            pl.BlockSpec((tokens, wide), lambda j: (0, j)),
+            pl.BlockSpec((feats // BLK, wide), lambda j: (0, j)),
+            pl.BlockSpec((feats // BLK, wide), lambda j: (0, j)),
+        ],
+        out_specs=(pl.BlockSpec((feats, wide), lambda j: (0, j)),) * 2,
+        compiler_params=pltpu.CompilerParams(vmem_limit_bytes=VMEM_LIMIT),
+        name="weight_grads",
+    )(xt, dg.reshape(tokens, ff), du.reshape(tokens, ff), kg, ku)
+    return summed.reshape(slots, feats), grad_w_gate, grad_w_up
 
 
 def expand(mask):
@@ -63,8 +352,9 @@
         P("dp", "tensor"),
         P("parts"),
     )
+    paired = mesh.shape["dp"] == 2 * CORES and mesh.shape["tensor"] == mesh.shape["dp"]
     return jax.shard_map(
-        local,
+        staged if paired else local,
         mesh=mesh,
         in_specs=placed,
         out_specs=(

time: 245 us -> 143 us (0.58)
  the two profiles are of different devices: /device:TPU:0 before, /device:TPU:25 now
where the time goes in v1:
time: 143 us
  Pallas kernels  142 us (99%)
    pallas_call x1, Pallas kernels, staged(): pl.pallas_call(gather_kernel, out_shape=(jax.ShapeDtypeStruct((STAGES, ro...  119 us
    pallas_call x1, Pallas kernels, staged(): pl.pallas_call(weight_kernel, grid=(ff // wide,), out_shape=(jax.ShapeDty...  22.6 us

profile of v1, /device:TPU:25, one launch (start us, length us, event | category | flops | bytes accessed | tf_op | source)
XLA Modules:
  0.0 143.1 jit_solution(14690697572287552637)
XLA Ops:
  0.6 119.1 %gather_and_input_grad.1 = (bf16[4,64,1024]{2,1,0:T(8,128)(2,1)}, bf16[2,4,2,64,4096]{4,3,2,1,0:T(8,128)(2,1)}, bf16[2,4,2,64,4096]{4,3,2,1,0:T(8,128)(2,1)}, bf...) custom-call(bf16[4,64,1024]{2,1,0:T(8,128)(2,1)} %bitcast.12, bf16[4,64,4096]{2,1,0:T(8,128)(2,1)} %bitcast.9, ...), custom_call_target="tpu_custom_call" | custom-call | tf_op jit(solution)/shard_map/gather_and_input_grad/pallas_call | solution.py:243
  119.7 0.0 copy-start
  119.7 22.6 %weight_grads.1 = (bf16[1024,4096]{1,0:T(8,128)(2,1)}, bf16[1024,4096]{1,0:T(8,128)(2,1)}) custom-call(bf16[1024,1024]{1,0:T(8,128)(2,1)} %get-tuple-element.12.xt, bf16[1024,4096]{1,0:T(8,128)(2,1)} %bitcast.7, bf16[1024,4096]{1,0:T(8,128)(2,1)} %bitcast.8, f32[8,4096]{1,0:T(8,128)} %get-tuple-element.15.kg, f32[8,4096]{1,0:T(8,128)} %get-tuple-element.16.ku), custom_call_target="tpu_custom_call" | custom-call | tf_op jit(solution)/shard_map/weight_grads/pallas_call | solution.py:280
  142.3 0.0 copy-done
  142.3 0.8 copy.13
Async XLA Ops:
  119.7 22.6 %copy-start = (bf16[4,64,1024]{2,1,0:T(8,128)(2,1)S(1)}, bf16[4,64,1024]{2,1,0:T(8,128)(2,1)}, u32[]{:S(2)}) copy-start(bf16[4,64,1024]{2,1,0:T(8,128)(2,1)} %get-tuple-element.11) | copy-start | bytes 1572868

commit v2 on v1

--- a/solution.py
+++ b/solution.py
@@ -9,17 +9,23 @@
 
 BLK = 128
 STAGES = 4
+EARLY = 2
 CORES = 2
 VMEM_LIMIT = 60 * 2**20
 MESH = pl.DeviceIdType.MESH
 NT = (((1,), (1,)), ((), ()))
 
 
+def cuts(feats):
+    half = feats // 2
+    return [(r, 0, feats) for r in range(STAGES - 1)] + [(STAGES - 1, 0, half), (STAGES - 1, half, half)]
+
+
 def gather_kernel(
     x_in, gate_in, up_in, dh_in, wg_in, wu_in, mg_in, mu_in, len_in,
-    summed, dg_out, du_out, xt_out, kg_out, ku_out,
-    dg, du, wg, wu, gate, up, dh, xs, term, part,
-    load_sem, w_sem, x_sem, xsend, xrecv, psend, precv, ssend, srecv, fsend, frecv, out_sem, rsend, rrecv,
+    summed, dg_out, du_out, pg_out, pu_out, xt_out, kg_out, ku_out,
+    dg, du, wg, wu, gate, up, dh, xs, xt, held, term, part,
+    load_sem, w_sem, x_sem, xsend, xrecv, psend, precv, ssend, srecv, fsend, frecv, out_sem, held_sem, rsend, rrecv,
 ):
     t = lax.axis_index("tensor")
     i = lax.axis_index("dp")
@@ -30,6 +36,7 @@
     pair = far * CORES + core
     stages, rows, ff = gate.shape
     feats = wg.shape[0]
+    pieces = cuts(feats)
 
     loads = []
     for r in range(stages):
@@ -117,42 +124,74 @@
 
     out_copies = []
 
-    def stage(where, r):
-        for k, (d, d_out) in enumerate(((dg, dg_out), (du, du_out))):
-            copy = pltpu.make_async_copy(d.at[where, r], d_out.at[where, r], out_sem.at[where, r, k])
-            copy.start()
-            out_copies.append(copy)
-        wide = min(256, feats)
-
-        @pl.loop(0, feats // wide)
+    def terms(where, first, last, low, many):
+        wide = min(256, many)
+        tall = (last - first) * CORES * rows
+
+        @pl.loop(0, many // wide)
         def _(n):
-            at = pl.ds(pl.multiple_of(n * wide, wide), wide)
+            at = pl.ds(pl.multiple_of(low + n * wide, wide), wide)
             total = lax.dot_general(
-                dg[where, r].reshape(CORES * rows, ff), wg[at, :], NT, preferred_element_type=jnp.float32
+                dg[where, first:last].reshape(tall, ff), wg[at, :], NT, preferred_element_type=jnp.float32
             )
             total = total + lax.dot_general(
-                du[where, r].reshape(CORES * rows, ff), wu[at, :], NT, preferred_element_type=jnp.float32
-            )
-            term[where, r, :, :, at] = total.astype(jnp.bfloat16).reshape(CORES, rows, wide)
-
-        for c in range(CORES):
-            owner = where * CORES + c
-
-            @pl.when(owner != t)
+                du[where, first:last].reshape(tall, ff), wu[at, :], NT, preferred_element_type=jnp.float32
+            )
+            term[where, first:last, :, :, at] = total.astype(jnp.bfloat16).reshape(
+                last - first, CORES, rows, wide
+            )
+
+        for q, (r, start, length) in enumerate(pieces):
+            if not (first <= r < last and low <= start < low + many):
+                continue
+            for c in range(CORES):
+                owner = where * CORES + c
+
+                @pl.when(owner != t)
+                def _():
+                    pltpu.make_async_remote_copy(
+                        src_ref=term.at[where, r, c, :, start : start + length],
+                        dst_ref=part.at[t, r, :, start : start + length],
+                        send_sem=rsend.at[owner, q],
+                        recv_sem=rrecv.at[t, q],
+                        device_id={"tensor": owner},
+                        device_id_type=MESH,
+                    ).start()
+
+    span = CORES * rows
+
+    def partial(k, d, p_out):
+        near, wide = stages * span, held.shape[2]
+        steps = ff // wide
+
+        def out(j):
+            cols = pl.ds(pl.multiple_of(j * wide, wide), wide)
+            return pltpu.make_async_copy(held.at[j % 2], p_out.at[:, cols], held_sem.at[k, j % 2])
+
+        @pl.loop(0, steps)
+        def _(j):
+            @pl.when(j >= 2)
             def _():
-                pltpu.make_async_remote_copy(
-                    src_ref=term.at[where, r, c],
-                    dst_ref=part.at[t, r],
-                    send_sem=rsend.at[owner, r],
-                    recv_sem=rrecv.at[t, r],
-                    device_id={"tensor": owner},
-                    device_id_type=MESH,
-                ).start()
+                out(j - 2).wait()
+
+            cols = pl.ds(pl.multiple_of(j * wide, wide), wide)
+            total = jnp.dot(
+                xt[:, :near], d[chip, :, :, :, cols].reshape(near, wide), preferred_element_type=jnp.float32
+            )
+            total = total + jnp.dot(
+                xt[:, near:], d[far, :EARLY, :, :, cols].reshape(EARLY * span, wide),
+                preferred_element_type=jnp.float32,
+            )
+            held[j % 2] = total.astype(jnp.bfloat16)
+            out(j).start()
+
+        for j in range(steps - 2, steps):
+            out(j).wait()
 
     for r in range(stages):
         for copy in s_copies[r]:
             copy.wait_recv()
-        stage(chip, r)
+    terms(chip, 0, stages, 0, feats)
 
     for r in range(stages):
         for copy in p_copies[r]:
@@ -172,25 +211,42 @@
             copy.start()
         for copy in f_copies[-1]:
             copy.wait_recv()
-        stage(far, r)
-        if r == stages - 2:
+        if r >= EARLY:
+            for k, (d, d_out) in enumerate(((dg, dg_out), (du, du_out))):
+                copy = pltpu.make_async_copy(d.at[far, r], d_out.at[r - EARLY], out_sem.at[r - EARLY, k])
+                copy.start()
+                out_copies.append(copy)
+        if r == EARLY - 1:
+            terms(far, 0, EARLY, 0, feats)
             own_x.wait()
             for copy in x_copies:
                 copy.wait_recv()
-            span = CORES * rows
-            for a in range(xs.shape[0]):
+            for at, where in enumerate((chip, far)):
                 for b in range(stages):
-                    at = (a * stages + b) * span
-                    xt_out[:, at : at + span] = xs[a, b].reshape(span, feats).T
+                    block = xs[where, b].reshape(span, feats).T
+                    if at == 0 or b < EARLY:
+                        first = (at * stages + b) * span
+                        xt[:, first : first + span] = block
+                    else:
+                        first = (b - EARLY) * span
+                        xt_out[:, first : first + span] = block
+            partial(0, dg, pg_out)
+        if EARLY <= r < stages - 1:
+            terms(far, r, r + 1, 0, feats)
+        if r == stages - 1:
+            terms(far, r, r + 1, 0, feats // 2)
+            terms(far, r, r + 1, feats // 2, feats // 2)
+        if r == EARLY:
+            partial(1, du, pu_out)
 
     for k in range(1, n_t):
-        for r in range(stages):
+        for q, (r, start, length) in enumerate(pieces):
             other = (t + k) % n_t
             copy = pltpu.make_async_remote_copy(
-                src_ref=term.at[other // CORES, r, other % CORES],
-                dst_ref=part.at[other, r],
-                send_sem=rsend.at[other, r],
-                recv_sem=rrecv.at[other, r],
+                src_ref=term.at[other // CORES, r, other % CORES, :, start : start + length],
+                dst_ref=part.at[other, r, :, start : start + length],
+                send_sem=rsend.at[other, q],
+                recv_sem=rrecv.at[other, q],
                 device_id={"tensor": other},
                 device_id_type=MESH,
             )
@@ -212,12 +268,13 @@
         copy.wait()
 
 
-def weight_kernel(xt, dg, du, kg, ku, out_g, out_u):
+def weight_kernel(xt, dg, du, pg, pu, kg, ku, out_g, out_u):
     feats = xt.shape[0]
     high = 256
-    for d, keep, out in ((dg, kg, out_g), (du, ku, out_u)):
+    for d, p, keep, out in ((dg, pg, kg, out_g), (du, pu, ku, out_u)):
         for a in range(feats // high):
             total = jnp.dot(xt[a * high : (a + 1) * high, :], d[...], preferred_element_type=jnp.float32)
+            total = total + p[a * high : (a + 1) * high, :].astype(jnp.float32)
             for b in range(high // BLK):
                 row = a * (high // BLK) + b
                 out[row * BLK : (row + 1) * BLK, :] = (
@@ -231,8 +288,10 @@
     chips = lengths.shape[0] // CORES
     rows = slots // STAGES
     n_t = chips * CORES
+    sent = len(cuts(feats))
     bf16, f32 = jnp.bfloat16, jnp.float32
-    tokens = chips * CORES * slots
+    late = chips // 2 * (STAGES - EARLY) * CORES * rows
+    wide = 512
 
     def cut(array):
         return array.reshape(STAGES, rows, array.shape[1])
@@ -240,18 +299,20 @@
     hbm = pl.BlockSpec(memory_space=pl.ANY)
     vmem = pl.BlockSpec(memory_space=pltpu.VMEM)
     dma = pltpu.SemaphoreType.DMA
-    summed, dg, du, xt, kg, ku = pl.pallas_call(
+    summed, dg, du, pg, pu, xt, kg, ku = pl.pallas_call(
         gather_kernel,
         out_shape=(
             jax.ShapeDtypeStruct((STAGES, rows, feats), bf16),
-            jax.ShapeDtypeStruct((chips, STAGES, CORES, rows, ff), bf16),
-            jax.ShapeDtypeStruct((chips, STAGES, CORES, rows, ff), bf16),
-            jax.ShapeDtypeStruct((feats, tokens), bf16),
+            jax.ShapeDtypeStruct((STAGES - EARLY, CORES, rows, ff), bf16),
+            jax.ShapeDtypeStruct((STAGES - EARLY, CORES, rows, ff), bf16),
+            jax.ShapeDtypeStruct((feats, ff), bf16),
+            jax.ShapeDtypeStruct((feats, ff), bf16),
+            jax.ShapeDtypeStruct((feats, late), bf16),
             jax.ShapeDtypeStruct((feats // BLK, ff), f32),
             jax.ShapeDtypeStruct((feats // BLK, ff), f32),
         ),
         in_specs=[hbm] * 6 + [vmem] * 2 + [pl.BlockSpec(memory_space=pltpu.SMEM)],
-        out_specs=(vmem, hbm, hbm, vmem, vmem, vmem),
+        out_specs=(vmem, hbm, hbm, hbm, hbm, vmem, vmem, vmem),
         scratch_shapes=[
             pltpu.VMEM((chips, STAGES, CORES, rows, ff), bf16),
             pltpu.VMEM((chips, STAGES, CORES, rows, ff), bf16),
@@ -261,12 +322,14 @@
             pltpu.VMEM((STAGES, rows, ff), bf16),
             pltpu.VMEM((STAGES, rows, ff), bf16),
             pltpu.VMEM((chips, STAGES, CORES, rows, feats), bf16),
+            pltpu.VMEM((feats, n_t * slots - late), bf16),
+            pltpu.VMEM((2, feats, wide), bf16),
             pltpu.VMEM((chips, STAGES, CORES, rows, feats), bf16),
             pltpu.VMEM((n_t, STAGES, rows, feats), bf16),
             dma((STAGES, 3)), dma((2,)), dma, dma((n_t - 1,)), dma((n_t - 1,)),
             dma((STAGES, 2)), dma((STAGES, 2)), dma((STAGES, 2)), dma((STAGES, 2)),
-            dma((STAGES, 2)), dma((STAGES, 2)), dma((chips, STAGES, 2)),
-            dma((n_t, STAGES)), dma((n_t, STAGES)),
+            dma((STAGES, 2)), dma((STAGES, 2)), dma((STAGES - EARLY, 2)), dma((2, 2)),
+            dma((n_t, sent)), dma((n_t, sent)),
         ],
         compiler_params=pltpu.CompilerParams(
             collective_id=0, has_side_effects=True, vmem_limit_bytes=VMEM_LIMIT
@@ -276,22 +339,24 @@
         cut(layer_input), cut(gate_pre), cut(up_pre), cut(d_hidden),
         w_gate, w_up, mask_gate, mask_up, lengths,
     )
-    wide = 512
+    wide = 1024
     grad_w_gate, grad_w_up = pl.pallas_call(
         weight_kernel,
         grid=(ff // wide,),
         out_shape=(jax.ShapeDtypeStruct((feats, ff), bf16),) * 2,
         in_specs=[
-            pl.BlockSpec((feats, tokens), lambda j: (0, 0)),
-            pl.BlockSpec((tokens, wide), lambda j: (0, j)),
-            pl.BlockSpec((tokens, wide), lambda j: (0, j)),
+            pl.BlockSpec((feats, late), lambda j: (0, 0)),
+            pl.BlockSpec((late, wide), lambda j: (0, j)),
+            pl.BlockSpec((late, wide), lambda j: (0, j)),
+            pl.BlockSpec((feats, wide), lambda j: (0, j)),
+            pl.BlockSpec((feats, wide), lambda j: (0, j)),
             pl.BlockSpec((feats // BLK, wide), lambda j: (0, j)),
             pl.BlockSpec((feats // BLK, wide), lambda j: (0, j)),
         ],
         out_specs=(pl.BlockSpec((feats, wide), lambda j: (0, j)),) * 2,
         compiler_params=pltpu.CompilerParams(vmem_limit_bytes=VMEM_LIMIT),
         name="weight_grads",
-    )(xt, dg.reshape(tokens, ff), du.reshape(tokens, ff), kg, ku)
+    )(xt, dg.reshape(late, ff), du.reshape(late, ff), pg, pu, kg, ku)
     return summed.reshape(slots, feats), grad_w_gate, grad_w_up
 
 

time: 143 us -> 133 us (0.930)
  Pallas kernels: 142 us -> 131 us
    pallas_call x1, Pallas kernels: 22.6 us -> 14.3 us  [staged(): pl.pallas_call(weight_kernel, grid=(ff // wide,), out_shape=(jax.ShapeDty...]
    pallas_call x1, Pallas kernels: 119 us -> 116 us  [staged(): pl.pallas_call(gather_kernel, out_shape=(jax.ShapeDtypeStruct((STAGES, ro...]
where the time goes in v2:
time: 133 us; the launch traced here: 132 us
  Pallas kernels  131 us (98%)
    pallas_call x1, Pallas kernels, staged(): pl.pallas_call(gather_kernel, out_shape=(jax.ShapeDtypeStruct((STAGES, ro...  116 us
    pallas_call x1, Pallas kernels, staged(): pl.pallas_call(weight_kernel, grid=(ff // wide,), out_shape=(jax.ShapeDty...  14.3 us

profile of v2, /device:TPU:25, one launch (start us, length us, event | category | flops | bytes accessed | tf_op | source)
XLA Modules:
  0.0 132.2 jit_solution(13317152925306142017)
XLA Ops:
  0.6 116.4 %gather_and_input_grad.1 = (bf16[4,64,1024]{2,1,0:T(8,128)(2,1)}, bf16[2,2,64,4096]{3,2,1,0:T(8,128)(2,1)}, bf16[2,2,64,4096]{3,2,1,0:T(8,128)(2,1)}, bf16[1024,...) custom-call(bf16[4,64,1024]{2,1,0:T(8,128)(2,1)} %bitcast.12, ...), custom_call_target="tpu_custom_call" | custom-call | tf_op jit(solution)/shard_map/gather_and_input_grad/pallas_call | solution.py:302
  117.1 0.0 copy-start
  117.1 14.3 %weight_grads.1 = (bf16[1024,4096]{1,0:T(8,128)(2,1)}, bf16[1024,4096]{1,0:T(8,128)(2,1)}) custom-call(bf16[1024,256]{1,0:T(8,128)(2,1)} %get-tuple-element.14.xt, bf16[256,4096]{1,0:T(8,128)(2,1)} %bitcast.10, bf16[256,4096]{1,0:T(8,128)(2,1)} %bitcast.11, bf16[1024,4096]{1,0:T(8,128)(2,1)} %get-tuple-element.17.pg, ...), custom_call_target="tpu_custom_call" | custom-call | tf_op jit(solution)/shard_map/weight_grads/pallas_call | solution.py:343
  131.4 0.0 copy-done
  131.4 0.8 copy.13
Async XLA Ops:
  117.1 14.3 %copy-start = (bf16[4,64,1024]{2,1,0:T(8,128)(2,1)S(1)}, bf16[4,64,1024]{2,1,0:T(8,128)(2,1)}, u32[]{:S(2)}) copy-start(bf16[4,64,1024]{2,1,0:T(8,128)(2,1)} %get-tuple-element.13) | copy-start | bytes 1572868
